TPU v7x, 32 devices: a whole 2x2x4 slice. The times are simulated.
32 devices in a mesh: row: 8 (over z, y), col: 4 (over x, core).
Axes of the slice: x: 2, y: 2, z: 4, core: 2. Of those that a mesh axis runs over, the one named last changes fastest.
Arguments:
- patches: bfloat16 [160, 480, 512], P('row', 'col'), may hold values from -6 to 6
- region_ids: int32 [160, 480], P('row', 'col'), may hold values from 0 to 8, as said below
- qkv_weight: float32 [512, 1536], replicated, may hold values from -0.25 to 0.25
- query_bias: float32 [512], replicated, may hold values from -3 to 3
- value_bias: float32 [512], replicated, may hold values from -3 to 3
- bias_table: float32 [361, 16], replicated, may hold values from -6 to 6
- proj_weight: float32 [512, 512], replicated, may hold values from -1.5 to 1.5
- proj_bias: float32 [512], replicated, may hold values from -3 to 3
- gain_one: float32 [512], replicated, may hold values from 0.1 to 1.9
- shift_one: float32 [512], replicated, may hold values from -3 to 3
- gain_two: float32 [512], replicated, may hold values from 0.1 to 1.9
- shift_two: float32 [512], replicated, may hold values from -3 to 3
- up_weight: float32 [512, 2048], replicated, may hold values from -0.25 to 0.25
- up_bias: float32 [2048], replicated, may hold values from -3 to 3
- down_weight: float32 [2048, 512], replicated, may hold values from -0.125 to 0.125
- down_bias: float32 [512], replicated, may hold values from -3 to 3
- cotangent: bfloat16 [160, 480, 512], P('row', 'col'), may hold values from -6 to 6
Outputs:
- block_out: bfloat16 [160, 480, 512], P('row', 'col')
- patches_grad: bfloat16 [160, 480, 512], P('row', 'col')
- qkv_weight_grad: float32 [512, 1536], replicated
- query_bias_grad: float32 [512], replicated
- value_bias_grad: float32 [512], replicated
- bias_table_grad: float32 [361, 16], replicated
- proj_weight_grad: float32 [512, 512], replicated
- proj_bias_grad: float32 [512], replicated
- gain_one_grad: float32 [512], replicated
- shift_one_grad: float32 [512], replicated
- gain_two_grad: float32 [512], replicated
- shift_two_grad: float32 [512], replicated
- up_weight_grad: float32 [512, 2048], replicated
- up_bias_grad: float32 [2048], replicated
- down_weight_grad: float32 [2048, 512], replicated
- down_bias_grad: float32 [512], replicated
Inputs may be any that keep to these rules, and one draw needn't show every extreme that they name: `region_ids`: the grid is tiled by pages whose sides are multiples of 10, aligned to the windows of the shifted grid, all pages of one column group of 120 columns alike. Within a page of h rows and w columns, at row r' and column c' of the page, id = 3 * band(r', h) + band(c', w) with band(x, n) = 0 for x < n - 10, 1 for n - 10 <= x < n - 5, 2 otherwise, the usual shifted-window mask; no window holds patches of two pages. A patch attends only to patches of its own window with the same id.
All inputs are finite; a program needn't handle non-finite values.
Results may differ from a plain program's by a relative error of at most 0.012.
The roundings to bfloat16 on the way count: a program that leaves them out, or rounds other values in their place, can miss the bound.
Values may be sent and summed in bfloat16 or wider, within the bound.
No kernel may reach another device: no remote copies, remote signals or barrier semaphores. Data moves between devices by JAX's collectives and lax.ppermute only.
A program may use at most 256 MiB of HBM per device.

v0:
```python
from functools import partial

import jax
import jax.numpy as jnp
from jax import lax
from jax.sharding import PartitionSpec as P

WIN = 10
SHIFT = 5


norm_eps = 1e-05
far_below = -1000000000.0


def from_behind(value, axis, steps):
    count = lax.axis_size(axis)
    pairs = [(source, (source + steps) % count) for source in range(count)]
    return lax.ppermute(value, axis, pairs)


def layer_norm(values, gain_vec, offset):
    center = values - jnp.mean(values, axis=-1, keepdims=True)
    spread = jnp.mean(center * center, axis=-1, keepdims=True)
    return center * lax.rsqrt(spread + norm_eps) * gain_vec + offset


def relative_index(window):
    places = jnp.arange(window * window, dtype=jnp.int32)
    prow = places // window
    pcol = places % window
    return (prow[:, None] - prow[None, :] + window - 1) * (2 * window - 1) + (
        pcol[:, None] - pcol[None, :] + window - 1
    )


def to_windows(grid):
    local_rows, local_cols = (grid.shape[0], grid.shape[1])
    trailing = grid.shape[2:]
    pieces = grid.reshape((local_rows // WIN, WIN, local_cols // WIN, WIN) + trailing)
    ordering = (0, 2, 1, 3) + tuple(range(4, pieces.ndim))
    return pieces.transpose(ordering).reshape(
        (local_rows // WIN * (local_cols // WIN), WIN * WIN) + trailing
    )


def from_windows(windows, local_rows, local_cols):
    trailing = windows.shape[2:]
    pieces = windows.reshape((local_rows // WIN, local_cols // WIN, WIN, WIN) + trailing)
    ordering = (0, 2, 1, 3) + tuple(range(4, pieces.ndim))
    return pieces.transpose(ordering).reshape((local_rows, local_cols) + trailing)


def roll_in(paired):
    upper = from_behind(paired[:, :SHIFT], "row", -1)
    paired = jnp.concatenate((paired[:, SHIFT:], upper), axis=1)
    leftmost = from_behind(paired[:, :, :SHIFT], "col", -1)
    return jnp.concatenate((paired[:, :, SHIFT:], leftmost), axis=2)


def roll_out(paired):
    lower = from_behind(paired[:, -SHIFT:], "row", 1)
    paired = jnp.concatenate((lower, paired[:, :-SHIFT]), axis=1)
    rightmost = from_behind(paired[:, :, -SHIFT:], "col", 1)
    return jnp.concatenate((rightmost, paired[:, :, :-SHIFT]), axis=2)


def body(
    patches,
    region_ids,
    qkv_weight,
    query_bias,
    value_bias,
    bias_table,
    proj_weight,
    proj_bias,
    gain_one,
    shift_one,
    gain_two,
    shift_two,
    up_weight,
    up_bias,
    down_weight,
    down_bias,
    cotangent,
):
    local_rows, local_cols, model_width = patches.shape
    head_count = bias_table.shape[1]
    head_size = model_width // head_count
    score_scale = head_size ** (-0.5)
    paired = roll_in(jnp.stack((patches, cotangent)))
    inputs = to_windows(paired[0]).reshape(-1, model_width).astype(jnp.float32)
    upstream_low = to_windows(paired[1]).reshape(-1, model_width)
    labels = to_windows(region_ids)
    window_count = labels.shape[0]
    onehot = (
        relative_index(WIN).reshape(-1)[:, None]
        == jnp.arange(bias_table.shape[0], dtype=jnp.int32)[None, :]
    ).astype(jnp.float32)
    position_bias = jnp.dot(onehot, bias_table, precision=lax.Precision.HIGHEST)
    position_bias = position_bias.reshape(WIN * WIN, WIN * WIN, head_count).transpose(2, 0, 1)
    same_region = labels[:, None, :, None] == labels[:, None, None, :]
    normed_one, norm_one_pull = jax.vjp(layer_norm, inputs, gain_one, shift_one)
    normed_one_low = normed_one.astype(jnp.bfloat16)
    qkv_low = qkv_weight.astype(jnp.bfloat16)
    joined = jnp.dot(normed_one_low, qkv_low, preferred_element_type=jnp.float32)
    joined = joined + jnp.concatenate((query_bias, jnp.zeros_like(query_bias), value_bias))
    joined_low = joined.astype(jnp.bfloat16).reshape(
        window_count, WIN * WIN, 3, head_count, head_size
    )
    queries = joined_low[:, :, 0]
    keys_low = joined_low[:, :, 1]
    values_low = joined_low[:, :, 2]

    def scores_of():
        raw = jnp.einsum("wqhd,wkhd->whqk", queries, keys_low, preferred_element_type=jnp.float32)
        return jnp.where(same_region, raw * score_scale + position_bias[None], far_below)

    scores = scores_of()
    row_max = jnp.max(scores, axis=-1, keepdims=True)
    exp_scores = jnp.exp(scores - row_max)
    row_total = jnp.sum(exp_scores, axis=-1, keepdims=True)
    probs = exp_scores / row_total
    log_total = row_max + jnp.log(row_total)
    probs_low = probs.astype(jnp.bfloat16)
    mixed_heads = jnp.einsum(
        "whqk,wkhd->wqhd", probs_low, values_low, preferred_element_type=jnp.float32
    )
    mixed_low = mixed_heads.reshape(-1, model_width).astype(jnp.bfloat16)
    proj_low = proj_weight.astype(jnp.bfloat16)
    branch = jnp.dot(mixed_low, proj_low, preferred_element_type=jnp.float32) + proj_bias
    middle = inputs + branch
    normed_two, norm_two_pull = jax.vjp(layer_norm, middle, gain_two, shift_two)
    normed_two_low = normed_two.astype(jnp.bfloat16)
    up_low = up_weight.astype(jnp.bfloat16)
    hidden = jnp.dot(normed_two_low, up_low, preferred_element_type=jnp.float32) + up_bias
    active, gelu_pull = jax.vjp(partial(jax.nn.gelu, approximate=False), hidden)
    active_low = active.astype(jnp.bfloat16)
    down_low = down_weight.astype(jnp.bfloat16)
    result = middle + jnp.dot(active_low, down_low, preferred_element_type=jnp.float32) + down_bias
    upstream = upstream_low.astype(jnp.float32)
    down_grad = jnp.dot(active_low.T, upstream_low, preferred_element_type=jnp.float32)
    down_bias_grad = jnp.sum(upstream, axis=0)
    active_grad = jnp.dot(upstream_low, down_low.T, preferred_element_type=jnp.float32)
    hidden_grad_low = gelu_pull(active_grad)[0].astype(jnp.bfloat16)
    up_grad = jnp.dot(normed_two_low.T, hidden_grad_low, preferred_element_type=jnp.float32)
    up_bias_grad = jnp.sum(hidden_grad_low.astype(jnp.float32), axis=0)
    normed_two_grad = jnp.dot(hidden_grad_low, up_low.T, preferred_element_type=jnp.float32)
    middle_grad, gain_two_grad, shift_two_grad = norm_two_pull(normed_two_grad)
    middle_grad = middle_grad + upstream
    branch_grad_low = middle_grad.astype(jnp.bfloat16)
    proj_grad = jnp.dot(mixed_low.T, branch_grad_low, preferred_element_type=jnp.float32)
    proj_bias_grad = jnp.sum(branch_grad_low.astype(jnp.float32), axis=0)
    mixed_grad_low = jnp.dot(
        branch_grad_low, proj_low.T, preferred_element_type=jnp.float32
    ).astype(jnp.bfloat16)
    mixed_grad_low = mixed_grad_low.reshape(window_count, WIN * WIN, head_count, head_size)
    probs_grad = jnp.einsum(
        "wqhd,wkhd->whqk", mixed_grad_low, values_low, preferred_element_type=jnp.float32
    )
    values_grad = jnp.einsum(
        "whqk,wqhd->wkhd", probs_low, mixed_grad_low, preferred_element_type=jnp.float32
    )
    probs_again = jnp.exp(scores_of() - log_total)
    score_grad = probs_again * (
        probs_grad - jnp.sum(probs_grad * probs_again, axis=-1, keepdims=True)
    )
    table_terms = jnp.sum(score_grad, axis=0).reshape(head_count, -1).T
    table_grad = jnp.dot(onehot.T, table_terms, precision=lax.Precision.HIGHEST)
    raw_grad_low = (score_grad * score_scale).astype(jnp.bfloat16)
    queries_grad = jnp.einsum(
        "whqk,wkhd->wqhd", raw_grad_low, keys_low, preferred_element_type=jnp.float32
    )
    keys_grad = jnp.einsum(
        "whqk,wqhd->wkhd", raw_grad_low, queries, preferred_element_type=jnp.float32
    )
    joined_grad_low = (
        jnp.stack((queries_grad, keys_grad, values_grad), axis=2)
        .astype(jnp.bfloat16)
        .reshape(-1, 3 * model_width)
    )
    qkv_grad = jnp.dot(normed_one_low.T, joined_grad_low, preferred_element_type=jnp.float32)
    joined_sums = jnp.sum(joined_grad_low.astype(jnp.float32), axis=0)
    query_bias_grad = joined_sums[:model_width]
    value_bias_grad = joined_sums[2 * model_width :]
    normed_one_grad = jnp.dot(joined_grad_low, qkv_low.T, preferred_element_type=jnp.float32)
    input_grad, gain_one_grad, shift_one_grad = norm_one_pull(normed_one_grad)
    input_grad = input_grad + middle_grad
    out_grid = from_windows(
        result.reshape(window_count, WIN * WIN, model_width), local_rows, local_cols
    )
    grad_grid = from_windows(
        input_grad.reshape(window_count, WIN * WIN, model_width), local_rows, local_cols
    )
    returned = roll_out(jnp.stack((out_grid.astype(jnp.bfloat16), grad_grid.astype(jnp.bfloat16))))
    summed = lax.psum(
        (
            qkv_grad,
            query_bias_grad,
            value_bias_grad,
            table_grad,
            proj_grad,
            proj_bias_grad,
            gain_one_grad,
            shift_one_grad,
            gain_two_grad,
            shift_two_grad,
            up_grad,
            up_bias_grad,
            down_grad,
            down_bias_grad,
        ),
        ("row", "col"),
    )
    return (
        returned[0],
        returned[1],
        summed[0],
        summed[1],
        summed[2],
        summed[3],
        summed[4],
        summed[5],
        summed[6],
        summed[7],
        summed[8],
        summed[9],
        summed[10],
        summed[11],
        summed[12],
        summed[13],
    )


def solution(mesh):
    placed = (
        P("row", "col", None),
        P("row", "col"),
        P(),
        P(),
        P(),
        P(),
        P(),
        P(),
        P(),
        P(),
        P(),
        P(),
        P(),
        P(),
        P(),
        P(),
        P("row", "col", None),
    )
    return jax.shard_map(
        body,
        mesh=mesh,
        in_specs=placed,
        out_specs=(
            P("row", "col", None),
            P("row", "col", None),
            P(),
            P(),
            P(),
            P(),
            P(),
            P(),
            P(),
            P(),
            P(),
            P(),
            P(),
            P(),
            P(),
            P(),
        ),
        check_vma=False,
    )
```

profile of v0, /device:TPU:0, one launch (start us, length us, event | category | flops | bytes accessed | tf_op | source)
XLA Modules:
  0.0 734.0 jit_solution(16205812543372571722)
XLA Ops:
  9.7 6.0 collective-permute-start
  16.5 7.7 %fusion.12 = f32[10000,16]{0,1:T(8,128)} fusion(f32[361,16]{0,1:T(8,128)S(1)} %copy-done, s32[10000]{0:T(1024)S(1)} %add.204), kind=kOutput, calls=%fused_computation.32 | convolution fusion | flops 696729984 | bytes 703104 | tf_op jit(solution)/shard_map/dot_general | solution.py:100
  29.9 12.4 %collective-permute-done = bf16[2,5,120,512]{3,2,1,0:T(8,128)(2,1)} collective-permute-done((bf16[2,5,120,512]{3,2,1,0:T(8,128)(2,1)}, bf16[2,5,120,512]{3,2,1,0:T(8,128)(2,1)}, u32[]{:S(2)}, u32[]{:S(2)}) %collective-permute-start) | collective-permute-done | bytes 1228832 | tf_op jit(solution)/shard_map/ppermute | solution.py:19
  51.8 6.8 reshape.304
  66.7 8.1 %copy.71 = f32[2,12,10,10,512]{4,3,2,1,0:T(8,128)} copy(f32[2,12,10,10,512]{4,3,1,2,0:T(8,128)} %bitcast.89) | data formatting | bytes 9830400 | tf_op jit(solution)/shard_map/convert_element_type | solution.py:92
  74.7 6.9 reshape.302
  81.7 9.3 %add_convert_fusion.1 = bf16[2400,1536]{1,0:T(8,128)(2,1)} fusion(f32[1536]{0:T(1024)S(1)} %pad_maximum_fusion.5, f32[2400,512]{1,0:T(8,128)} %reshape.302, f32[512]{0:T(512)S(1)} %copy-done.51, f32[512]{0:T(512)S(1)} %copy-done.44, f32[2400]{0:T(1024)S(1)} %rsqrt.23, f32[2400]{0:T(1024)S(1)} %div.63, f32[512,1536]{1,0:T(8,128)} %param.19), kind=kOutput, calls=%fused_computation.33 | convolution fusion | flops 3789176832 | bytes 15463168 | tf_op jit(solution)/shard_map/dot_general | solution.py:106
  91.0 10.1 %copy.74 = bf16[2400,1536]{0,1:T(8,128)(2,1)} copy(bf16[2400,1536]{1,0:T(8,128)(2,1)} %add_convert_fusion.1) | data formatting | bytes 14745600 | tf_op jit(solution)/shard_map/convert_element_type | solution.py:108
  101.1 17.6 %reshape.297 = bf16[24,100,3,16,32]{1,0,4,3,2:T(8,128)(2,1)} reshape(bf16[2400,1536]{0,1:T(8,128)(2,1)} %copy.74) | data formatting | bytes 14745600 | tf_op jit(solution)/shard_map/reshape | solution.py:108
  123.3 11.9 %fusion.60 = (f32[24,16,100]{2,1,0:T(8,128)S(1)}, f32[24,16,100,100]{2,3,1,0:T(8,128)}) fusion(f32[16,100,100]{1,2,0:T(8,128)} %copy.81, bf16[24,100,1,16,32]{1,0,4,3,2:T(8,128)(2,1)S(1)} %get-tuple-element.48, bf16[24,100,1,16,32]{1,0,4,3,2:T(8,128)(2,1)S(1)} %get-tuple-element.47, pred[24,100,100]{1,2,0:T(8,128)(4,1)} %broadcast_compare_fusion), kind=kOutput, calls=%fused_computation.131 | convolution fusion | flops 261081600 | bytes 21308800 | tf_op jit(solution)/shard_map/wqhd,wkhd->whqk/dot_general | solution.py:116
  135.2 11.4 %fusion.8 = f32[24,16,100]{2,1,0:T(8,128)S(1)} fusion(f32[24,16,100,100]{2,3,1,0:T(8,128)} %get-tuple-element.58, f32[24,16,100]{2,1,0:T(8,128)S(1)} %get-tuple-element.57), kind=kLoop, calls=%fused_computation.29 | loop fusion | flops 7641600 | bytes 15667200 | tf_op jit(solution)/shard_map/reduce_sum | solution.py:122
  148.1 6.9 divide_convert_fusion
  190.5 50.6 %multiply_convert_fusion.1 = (bf16[2400,2048]{1,0:T(8,128)(2,1)}, f32[2400,2048]{1,0:T(8,128)}, f32[2400,2048]{1,0:T(8,128)}) fusion(f32[2048]{0:T(1024)S(1)} %copy-done.55, f32[512,2048]{1,0:T(8,128)S(1)} %copy-done.53, f32[2400,512]{1,0:T(8,128)S(1)} %get-tuple-element.60, f32[512]{0:T(512)S(1)} %copy-done.56, f32[512]{0:T(512)S(1)} %copy-done.46, ...), kind=kOutput, calls=%fused_computation.13 | convolution fusion | flops 5364760576 | bytes 58292992 | tf_op jit(solution)/shard_map/dot_general | solution.py:136
  241.1 25.8 %convert_reduce_fusion = (f32[2048]{0:T(1024)}, bf16[2400,2048]{1,0:T(8,128)(2,1)}) fusion(f32[2400,2048]{1,0:T(8,128)} %get-tuple-element.45, bf16[2400,512]{1,0:T(8,128)(2,1)} %reshape_reshape.2, f32[2048,512]{1,0:T(8,128)} %param.31, f32[2400,2048]{1,0:T(8,128)} %get-tuple-element.61, f32[2048]{0:T(1024)S(1)} %copy-done.55), kind=kOutput, calls=%fused_computation.11 | convolution fusion | flops 5117769728 | bytes 55820288 | tf_op jit(solution)/shard_map/dot_general | solution.py:144
  266.9 11.8 %fusion.53 = f32[512,2048]{1,0:T(8,128)} fusion(bf16[2400,2048]{1,0:T(8,128)(2,1)} %get-tuple-element.67, f32[2400,512]{1,0:T(8,128)S(1)} %get-tuple-element.60, f32[512]{0:T(512)S(1)} %copy-done.56, f32[512]{0:T(512)S(1)} %copy-done.46, f32[2400]{0:T(1024)S(1)} %fusion.49, f32[2400]{0:T(1024)S(1)} %broadcast_multiply_fusion.1), kind=kOutput, calls=%fused_computation.126 | convolution fusion | flops 5039308800 | bytes 18963200 | tf_op jit(solution)/shard_map/dot_general | solution.py:146
  278.7 11.3 %multiply_reduce_fusion.2 = (f32[512]{0:T(512)}, f32[2400]{0:T(1024)S(1)}, f32[512]{0:T(512)}, f32[2400,512]{1,0:T(8,128)S(1)}) fusion(f32[2400,512]{1,0:T(8,128)S(1)} %get-tuple-element.60, f32[2400]{0:T(1024)S(1)} %fusion.49, f32[2400]{0:T(1024)S(1)} %broadcast_multiply_fusion.1, f32[512]{0:T(512)S(1)} %copy-done.46, ...), kind=kOutput, calls=%fused_computation.50 | convolution fusion | flops 5044040192 | bytes 23890048 | tf_op jit(solution)/shard_map/dot_general | solution.py:148
  309.2 12.1 %fusion.27 = bf16[24,100,1,16,32]{1,4,3,0,2:T(8,128)(2,1)} fusion(bf16[24,16,100,100]{2,3,1,0:T(8,128)(2,1)} %divide_convert_fusion, bf16[24,100,16,32]{1,0,3,2:T(8,128)(2,1)} %reshape.300), kind=kOutput, calls=%fused_computation.76 | convolution fusion | flops 245760000 | bytes 12595200 | tf_op jit(solution)/shard_map/whqk,wqhd->wkhd/dot_general | solution.py:161
  321.3 11.2 %fusion.22 = f32[24,16,100,100]{2,3,1,0:T(8,128)} fusion(bf16[24,100,1,16,32]{1,0,4,3,2:T(8,128)(2,1)S(1)} %copy-done.7, bf16[24,100,16,32]{1,0,3,2:T(8,128)(2,1)} %reshape.300), kind=kOutput, calls=%fused_computation.71 | convolution fusion | flops 245760000 | bytes 20275200 | tf_op jit(solution)/shard_map/wqhd,wkhd->whqk/dot_general | solution.py:158
  332.5 35.6 %fusion.62 = (f32[16,100,100]{1,2,0:T(8,128)}, f32[24,16,100,100]{2,3,1,0:T(8,128)}) fusion(f32[24,16,100,100]{2,3,1,0:T(8,128)} %fusion.22, f32[24,16,100,100]{2,3,1,0:T(8,128)} %get-tuple-element.58, f32[24,16,100]{2,1,0:T(8,128)S(1)} %copy-done.28), kind=kOutput, calls=%fused_computation.133 | output fusion | flops 22918500 | bytes 46873600 | tf_op jit(solution)/shard_map/sub | solution.py:166
  368.2 15.0 %fusion.31 = bf16[24,100,1,16,32]{1,4,3,0,2:T(8,128)(2,1)} fusion(f32[24,16,100,100]{2,3,1,0:T(8,128)} %get-tuple-element.65, bf16[24,100,1,16,32]{1,0,4,3,2:T(8,128)(2,1)} %copy-done.14), kind=kOutput, calls=%fused_computation.78 | convolution fusion | flops 253440000 | bytes 20275200 | tf_op jit(solution)/shard_map/whqk,wqhd->wkhd/dot_general | solution.py:174
  383.2 10.1 %fusion.30 = bf16[24,100,1,16,32]{1,4,3,0,2:T(8,128)(2,1)} fusion(f32[24,16,100,100]{2,3,1,0:T(8,128)} %get-tuple-element.65, bf16[24,100,1,16,32]{1,0,4,3,2:T(8,128)(2,1)S(1)} %copy-done.13), kind=kOutput, calls=%fused_computation.77 | convolution fusion | flops 253440000 | bytes 20275200 | tf_op jit(solution)/shard_map/whqk,wkhd->wqhd/dot_general | solution.py:171
  405.4 9.7 %fusion.65 = f32[2048,512]{1,0:T(8,128)} fusion(bf16[2400,2048]{1,0:T(8,128)(2,1)} %get-tuple-element.44, bf16[2400,512]{1,0:T(8,128)(2,1)S(1)} %copy-done.10), kind=kOutput, calls=%fused_computation.136 | convolution fusion | flops 5033164800 | bytes 16482304 | tf_op jit(solution)/shard_map/dot_general | solution.py:142
  415.1 6.9 convert_reduce_fusion.1
  422.0 18.3 %copy.92 = bf16[24,100,3,16,32]{1,0,4,3,2:T(8,128)(2,1)} copy(bf16[24,100,3,16,32]{1,4,3,0,2:T(8,128)(2,1)} %get-tuple-element.39) | data formatting | bytes 14745600 | tf_op jit(solution)/shard_map/convert_element_type | solution.py:179
  440.2 15.8 %convert_element_type.169 = bf16[2400,1536]{0,1:T(8,128)(2,1)} reshape(bf16[24,100,3,16,32]{1,0,4,3,2:T(8,128)(2,1)} %copy.92) | data formatting | bytes 14745600 | tf_op jit(solution)/shard_map/convert_element_type | solution.py:179
  456.1 9.8 %fusion.63 = f32[512,1536]{1,0:T(8,128)} fusion(bf16[2400,512]{1,0:T(8,128)(2,1)} %convert_element_type.175, bf16[2400,1536]{0,1:T(8,128)(2,1)} %convert_element_type.169), kind=kOutput, calls=%fused_computation.134 | convolution fusion | flops 3774873600 | bytes 12976128 | tf_op jit(solution)/shard_map/dot_general | solution.py:182
  466.6 10.9 %add_convert_fusion.4 = bf16[2400,512]{1,0:T(8,128)(2,1)} fusion(f32[2400,512]{1,0:T(8,128)} %copy-done.4, bf16[2400,2048]{1,0:T(8,128)(2,1)} %get-tuple-element.44, f32[512]{0:T(512)S(1)} %copy-done.57, f32[2048,512]{1,0:T(8,128)} %param.31), kind=kOutput, calls=%fused_computation.57 | convolution fusion | flops 5037899776 | bytes 21399552 | tf_op jit(solution)/shard_map/dot_general | solution.py:140
  487.6 5.8 convert_element_type.162
  493.5 12.4 %multiply_reduce_fusion.3 = (f32[512]{0:T(512)S(1)}, f32[2400]{0:T(1024)S(1)}, f32[512]{0:T(512)S(1)}, f32[2400,512]{1,0:T(8,128)S(1)}) fusion(f32[2400,512]{1,0:T(8,128)} %reshape.302, f32[2400]{0:T(1024)S(1)} %copy-done.37, f32[2400]{0:T(1024)S(1)} %copy-done.35, f32[512]{0:T(512)S(1)} %copy-done.45, bf16[2400,1536]{0,1:T(8,128)(2,1)} %convert_element_type.169, ...), kind=kOutput, calls=%fused_computation.51 | convolution fusion | flops 3785487104 | bytes 20383872 | tf_op jit(solution)/shard_map/dot_general | solution.py:186
  538.4 36.0 %collective-permute-done.2 = bf16[2,5,120,512]{3,2,1,0:T(8,128)(2,1)S(1)} collective-permute-done((bf16[2,5,120,512]{3,2,1,0:T(8,128)(2,1)}, bf16[2,5,120,512]{3,2,1,0:T(8,128)(2,1)S(1)}, u32[]{:S(2)}, u32[]{:S(2)}) %collective-permute-start.2) | collective-permute-done | bytes 1228832 | tf_op jit(solution)/shard_map/ppermute | solution.py:19
  583.3 38.5 %all-reduce = (f32[512]{0:T(512)}, f32[512]{0:T(512)}, f32[361,16]{0,1:T(8,128)}, f32[512]{0:T(512)}, f32[512]{0:T(512)}, /*index=5*/f32[512]{0:T(512)}, f32[512...) all-reduce(f32[512]{0:T(512)S(1)} %slice.73, ...), channel_id=1, replica_groups=mesh['row'=8,'col'=4] {'row','col'}, use_global_device_ids=true, to_apply=%region_13.14 | all-reduce | flops 11920 | bytes 95360 | tf_op jit(solution)/shard_map/psum | solution.py:196
  628.0 89.0 %all-reduce.4.cloned.1.call-done = (f32[512,1536]{1,0:T(8,128)}, f32[512,512]{1,0:T(8,128)}, f32[512,2048]{1,0:T(8,128)}, f32[2048,512]{1,0:T(8,128)}) async-done(((f32[512,1536]{1,0:T(8,128)}, f32[512,512]{1,0:T(8,128)}, f32[512,2048]{1,0:T(8,128)}, f32[2048,512]{1,0:T(8,128)}), (f32[512,1536]{1,0:T(8,128)}, f32[512,512]{1,0:T(8,128)}, f32[512,2048]{1,0:T(8,128)}, ...) | async-done | bytes 12582928 | tf_op jit(solution)/shard_map/psum | solution.py:196
  (204 shorter events, 167.4 us)
Async XLA Ops:
  7.2 709.7 %all-reduce.4.cloned.1.call-start = ((), (), s32[]{:S(2)}) async-start(), calls=%async_computation | async-start | bytes 25165824 | tf_op jit(solution)/shard_map/psum | solution.py:196
  9.7 32.6 %collective-permute-start = (bf16[2,5,120,512]{3,2,1,0:T(8,128)(2,1)}, bf16[2,5,120,512]{3,2,1,0:T(8,128)(2,1)}, u32[]{:S(2)}, u32[]{:S(2)}) collective-permute-start(bf16[2,5,120,512]{3,2,1,0:T(8,128)(2,1)} %pad_maximum_fusion.2), channel_id=1, source_target_pairs={{0,28},{4,0},{8,4},{12,8},{16,12},{20,16},{24,20},{28,24},{1,29},{... | collective-permute-start | bytes 3686408 | tf_op jit(solution)/shard_map/ppermute | solution.py:19
  16.2 10.8 %copy-start.47 = (f32[512]{0:T(512)S(1)}, f32[512]{0:T(512)}, u32[]{:S(2)}) copy-start(f32[512]{0:T(512)} %param.21) | copy-start | bytes 6148
  16.2 10.8 %copy-start.48 = (f32[512]{0:T(512)S(1)}, f32[512]{0:T(512)}, u32[]{:S(2)}) copy-start(f32[512]{0:T(512)} %param.20) | copy-start | bytes 6148
  16.5 11.7 %copy-start.20 = (bf16[20,120,512]{2,1,0:T(8,128)(2,1)S(1)}, bf16[20,120,512]{2,1,0:T(8,128)(2,1)}, u32[]{:S(2)}) copy-start(bf16[20,120,512]{2,1,0:T(8,128)(2,1)} %param.33) | copy-start | bytes 7372804
  43.2 5.0 collective-permute-start.1
  66.5 15.2 %copy-start.36 = (f32[2400]{0:T(1024)}, f32[2400]{0:T(1024)S(1)}, u32[]{:S(2)}) copy-start(f32[2400]{0:T(1024)S(1)} %rsqrt.23) | copy-start | bytes 28804
  66.6 15.0 %copy-start.34 = (f32[2400]{0:T(1024)}, f32[2400]{0:T(1024)S(1)}, u32[]{:S(2)}) copy-start(f32[2400]{0:T(1024)S(1)} %div.63) | copy-start | bytes 28804
  123.3 11.9 %copy-start.12 = (bf16[24,100,1,16,32]{1,0,4,3,2:T(8,128)(2,1)}, bf16[24,100,1,16,32]{1,0,4,3,2:T(8,128)(2,1)S(1)}, u32[]{:S(2)}) copy-start(bf16[24,100,1,16,32]{1,0,4,3,2:T(8,128)(2,1)S(1)} %get-tuple-element.48) | copy-start | bytes 7372804
  123.3 11.9 %copy-start.14 = (bf16[24,100,1,16,32]{1,0,4,3,2:T(8,128)(2,1)}, bf16[24,100,1,16,32]{1,0,4,3,2:T(8,128)(2,1)S(1)}, u32[]{:S(2)}) copy-start(bf16[24,100,1,16,32]{1,0,4,3,2:T(8,128)(2,1)S(1)} %get-tuple-element.47) | copy-start | bytes 7372804
  123.3 47.3 %copy-start.6 = (bf16[24,100,1,16,32]{1,0,4,3,2:T(8,128)(2,1)}, bf16[24,100,1,16,32]{1,0,4,3,2:T(8,128)(2,1)S(1)}, u32[]{:S(2)}) copy-start(bf16[24,100,1,16,32]{1,0,4,3,2:T(8,128)(2,1)S(1)} %get-tuple-element.46) | copy-start | bytes 7372804
  135.2 12.8 %copy-start.3 = (f32[24,16,100,100]{2,3,1,0:T(8,128)S(1)}, f32[24,16,100,100]{2,3,1,0:T(8,128)}, u32[]{:S(2)}) copy-start(f32[24,16,100,100]{2,3,1,0:T(8,128)} %get-tuple-element.58) | copy-start | bytes 46080004
  186.5 103.6 %copy-start.4 = (f32[2400,512]{1,0:T(8,128)}, f32[2400,512]{1,0:T(8,128)S(1)}, u32[]{:S(2)}) copy-start(f32[2400,512]{1,0:T(8,128)S(1)} %get-tuple-element.60) | copy-start | bytes 14745604
  187.5 53.6 %copy-start.30 = (f32[2400]{0:T(1024)}, f32[2400]{0:T(1024)S(1)}, u32[]{:S(2)}) copy-start(f32[2400]{0:T(1024)S(1)} %multiply_reduce_fusion.6) | copy-start | bytes 28804
  266.9 11.8 %copy-start.54 = (f32[512,2048]{1,0:T(8,128)S(1)}, f32[512,2048]{1,0:T(8,128)}, u32[]{:S(2)}) copy-start(f32[512,2048]{1,0:T(8,128)} %param.29) | copy-start | bytes 12582916
  278.7 11.3 %copy-start.31 = (f32[2400]{0:T(1024)S(1)}, f32[2400]{0:T(1024)}, u32[]{:S(2)}) copy-start(f32[2400]{0:T(1024)} %copy-done.30) | copy-start | bytes 28804
  309.2 12.1 %copy-start.7 = (bf16[24,100,1,16,32]{1,0,4,3,2:T(8,128)(2,1)S(1)}, bf16[24,100,1,16,32]{1,0,4,3,2:T(8,128)(2,1)}, u32[]{:S(2)}) copy-start(bf16[24,100,1,16,32]{1,0,4,3,2:T(8,128)(2,1)} %copy-done.6) | copy-start | bytes 7372804
  321.3 11.2 %copy-start.28 = (f32[24,16,100]{2,1,0:T(8,128)S(1)}, f32[24,16,100]{2,1,0:T(8,128)}, u32[]{:S(2)}) copy-start(f32[24,16,100]{2,1,0:T(8,128)} %log_add_fusion) | copy-start | bytes 460804
  368.2 15.0 %copy-start.13 = (bf16[24,100,1,16,32]{1,0,4,3,2:T(8,128)(2,1)S(1)}, bf16[24,100,1,16,32]{1,0,4,3,2:T(8,128)(2,1)}, u32[]{:S(2)}) copy-start(bf16[24,100,1,16,32]{1,0,4,3,2:T(8,128)(2,1)} %copy-done.12) | copy-start | bytes 7372804
  383.1 10.1 %copy-start.29 = (f32[2,12,10,10]{3,1,2,0:T(8,128)S(1)}, f32[2,12,10,10]{3,1,2,0:T(8,128)}, u32[]{:S(2)}) copy-start(f32[2,12,10,10]{3,1,2,0:T(8,128)} %get-tuple-element.53) | copy-start | bytes 28804
  383.1 10.1 %copy-start.45 = (f32[512]{0:T(512)S(1)}, f32[512]{0:T(512)}, u32[]{:S(2)}) copy-start(f32[512]{0:T(512)} %param.25) | copy-start | bytes 6148
  487.6 18.3 %slice-start = ((s8[4915200]{0:T(1024)(128)(4,1)}), s8[720896]{0:T(1024)(128)(4,1)S(1)}, s32[]{:S(2)}) async-start(s8[4915200]{0:T(1024)(128)(4,1)} %bitcast.90), calls=%async_computation.1 | async-start | bytes 1441792
  493.5 12.4 %copy-start.33 = (f32[2400]{0:T(1024)S(1)}, f32[2400]{0:T(1024)}, u32[]{:S(2)}) copy-start(f32[2400]{0:T(1024)} %copy-done.32) | copy-start | bytes 28804
  493.5 12.4 %slice-start.1 = ((s8[4915200]{0:T(1024)(128)(4,1)}), s8[4194304]{0:T(1024)(128)(4,1)S(1)}, s32[]{:S(2)}) async-start(s8[4915200]{0:T(1024)(128)(4,1)} %bitcast.90), calls=%async_computation.2 | async-start | bytes 8388608
  531.8 42.6 %collective-permute-start.2 = (bf16[2,5,120,512]{3,2,1,0:T(8,128)(2,1)}, bf16[2,5,120,512]{3,2,1,0:T(8,128)(2,1)S(1)}, u32[]{:S(2)}, u32[]{:S(2)}) collective-permute-start(bf16[2,5,120,512]{3,2,1,0:T(8,128)(2,1)} %slice.85), channel_id=1, source_target_pairs={{0,4},{4,8},{8,12},{12,16},{16,20},{20,24},{24,28},{28,0},{1,5},{5... | collective-permute-start | bytes 3686408 | tf_op jit(solution)/shard_map/ppermute | solution.py:19
  535.0 43.1 %copy-start.39 = (s32[10000]{0:T(1024)S(1)}, s32[10000]{0:T(1024)}, u32[]{:S(2)}) copy-start(s32[10000]{0:T(1024)} %copy-done.38) | copy-start | bytes 120004
  535.2 39.2 %copy-start.8 = (bf16[2,15,120,512]{3,2,1,0:T(8,128)(2,1)S(1)}, bf16[2,15,120,512]{3,2,1,0:T(8,128)(2,1)}, u32[]{:S(2)}) copy-start(bf16[2,15,120,512]{3,2,1,0:T(8,128)(2,1)} %slice.86) | copy-start | bytes 11059204
  538.3 44.9 %copy-start.42 = (f32[512]{0:T(512)S(1)}, f32[512]{0:T(512)}, u32[]{:S(2)}) copy-start(f32[512]{0:T(512)} %get-tuple-element.36) | copy-start | bytes 6148
  538.3 44.9 %copy-start.43 = (f32[2048]{0:T(1024)S(1)}, f32[2048]{0:T(1024)}, u32[]{:S(2)}) copy-start(f32[2048]{0:T(1024)} %get-tuple-element.66) | copy-start | bytes 24580
  538.3 44.9 %copy-start.49 = (f32[512]{0:T(512)S(1)}, f32[512]{0:T(512)}, u32[]{:S(2)}) copy-start(f32[512]{0:T(512)} %get-tuple-element.16) | copy-start | bytes 6148
  538.4 44.9 %copy-start.50 = (f32[512]{0:T(512)S(1)}, f32[512]{0:T(512)}, u32[]{:S(2)}) copy-start(f32[512]{0:T(512)} %get-tuple-element.20) | copy-start | bytes 6148
  574.5 47.3 %collective-permute-start.3 = (bf16[2,20,5,512]{3,2,1,0:T(8,128)(2,1)S(1)}, bf16[2,20,5,512]{3,2,1,0:T(8,128)(2,1)S(1)}, u32[]{:S(2)}, u32[]{:S(2)}) collective-permute-start(bf16[2,20,5,512]{3,2,1,0:T(8,128)(2,1)S(1)} %pad_maximum_fusion.3), channel_id=1, source_target_pairs={{0,1},{1,2},{2,3},{3,0},{4,5},{5,6},{6,7},{7,4},{8,9},{9,10},{10,1... | collective-permute-start | bytes 614408 | tf_op jit(solution)/shard_map/ppermute | solution.py:19
  (33 other events, 174.0 us)
Sparse Core Ops, SparseCore 0:
  466.0 250.8 all-reduce.3
where the time goes:
time: 742 us; the launch traced here: 734 us
  matrix products  241 us (32%)
  local copies, waits for them, and re-layouts  187 us (25%)
  waiting for transfers between devices  140 us (19%)
  other arithmetic  103 us (14%)
  blocking collectives  38.5 us (5%)
  between operations  15 us (2%)
  starting transfers between devices  10.5 us (1%)
    psum x1, waiting for transfers between devices, body(): lax.psum((qkv_grad, query_bias_grad, value_bias_grad, table_grad, proj_gr...  89 us
    ppermute x4, waiting for transfers between devices, from_behind(): return lax.ppermute(value, axis, pairs)  50.6 us
    dot_general x1, matrix products, body(): jnp.dot(normed_two_low, up_low, preferred_element_type=jnp.float32)  50.6 us
    psum x1, blocking collectives, body(): lax.psum((qkv_grad, query_bias_grad, value_bias_grad, table_grad, proj_gr...  38.5 us
    sub x1, other arithmetic, body(): probs_grad - jnp.sum(probs_grad * probs_again, axis=-1, keepdims=True)  35.6 us
    convert_element_type x2, local copies, waits for them, and re-layouts, body(): joined_grad_low = jnp.stack((queries_grad, keys_grad, values_grad), axis=...  34.1 us
    dot_general x1, matrix products, body(): jnp.dot(upstream_low, down_low.T, preferred_element_type=jnp.float32)  25.8 us
    convert_element_type x3, local copies, waits for them, and re-layouts, body(): inputs = to_windows(paired[0]).reshape(-1, model_width).astype(jnp.float32)  21.8 us
  transfers between devices with their start and end apart: 5, of which 4 were waited for; matrix products, arithmetic and copies ran while one was open for 13% of the time, Pallas kernels for 0%

commit v1 on v0

v1 whole, which is shorter than its diff:
```python
import functools

import jax
import jax.numpy as jnp
from jax import lax
from jax.experimental import pallas as pl
from jax.experimental.pallas import tpu as pltpu
from jax.sharding import PartitionSpec as P

WIN = 10
SHIFT = 5
PLACES = WIN * WIN
PAD = 104
GROUP = 4
ROWS = GROUP * PAD
SLAB = 32
FF_PARTS = 4

norm_eps = 1e-05
far_below = -1000000000.0
LOG2E = 1.4426950408889634
bf16 = jnp.bfloat16
f32 = jnp.float32


def dot(left, right, left_dim=1, right_dim=0):
    return lax.dot_general(
        left, right, (((left_dim,), (right_dim,)), ((), ())), preferred_element_type=f32
    )


def whole(array):
    count = len(array.shape)
    return pl.BlockSpec(array.shape, lambda *ids: (0,) * count)


def params():
    return pltpu.CompilerParams(vmem_limit_bytes=60 * 2**20)


def norm_parts(values):
    center = values - jnp.mean(values, axis=-1, keepdims=True)
    rstd = lax.rsqrt(jnp.mean(center * center, axis=-1, keepdims=True) + norm_eps)
    return center * rstd, rstd


def norm_pull(grad, unit, rstd, gain):
    scaled = grad * gain
    return rstd * (
        scaled
        - jnp.mean(scaled, axis=-1, keepdims=True)
        - unit * jnp.mean(scaled * unit, axis=-1, keepdims=True)
    )


def head_masks():
    lane = lax.broadcasted_iota(jnp.int32, (1, 128), 1) // 32
    return [(lane == head).astype(f32).astype(bf16) for head in range(4)]


def spread_heads(tile):
    return jnp.concatenate([tile * mask for mask in head_masks()], axis=0)


def gather_heads(stacked):
    lane = lax.broadcasted_iota(jnp.int32, (PAD, 128), 1) // 32
    out = stacked[0:PAD]
    for head in range(1, 4):
        out = jnp.where(lane == head, stacked[PAD * head : PAD * (head + 1)], out)
    return out


def window_rows(upper, lower, col, last_start):
    width = upper.shape[-1]
    first = col * WIN + SHIFT
    start = pl.multiple_of(jnp.minimum(first // 16 * 16, last_start), 16)
    offset = first - start
    half = upper.shape[0] * SLAB
    slab = jnp.concatenate(
        (
            upper[:, pl.ds(start, SLAB), :].reshape(half, width),
            lower[:, pl.ds(start, SLAB), :].reshape(half, width),
        ),
        axis=0,
    )
    place = lax.broadcasted_iota(jnp.int32, (PAD, 2 * half), 0)
    lane = lax.broadcasted_iota(jnp.int32, (PAD, 2 * half), 1)
    prow = (place * 205) >> 11
    target = place + (SLAB - WIN) * prow + offset
    hot = ((lane == target) & (place < PLACES)).astype(f32).astype(bf16)
    return dot(hot, slab)


def forward_kernel(
    last_start, upper, lower, label_row, label_col, bias, qkv, qkv_bias, proj, proj_bias, gain_one, shift_one,
    gain_two, shift_two, inputs, normed_one, joined, probs, mixed, middle, normed_two, rows_s, joined_s, mixed_s,
):
    part = pl.program_id(1)

    def load(window, _):
        at = pl.ds(pl.multiple_of(window * PAD, 8), PAD)
        rows_s[at, :] = window_rows(upper, lower, part * GROUP + window, last_start)
        return 0

    lax.fori_loop(0, GROUP, load, 0)
    rows = rows_s[...]
    inputs[...] = rows.astype(bf16)
    unit, _ = norm_parts(rows)
    normed = (unit * gain_one[...] + shift_one[...]).astype(bf16)
    normed_one[...] = normed
    joined_s[...] = dot(normed, qkv[...]) + qkv_bias[...]

    def attend(window, _):
        at = pl.ds(pl.multiple_of(window * PAD, 8), PAD)
        joined[window] = joined_s[at, :].astype(bf16)
        masked = jnp.where(label_col[window] == label_row[window], 0.0, far_below)
        for tile in range(4):
            lanes = 128 * tile
            queries = joined_s[at, lanes : lanes + 128].astype(bf16)
            keys = joined_s[at, 512 + lanes : 640 + lanes].astype(bf16)
            values = joined_s[at, 1024 + lanes : 1152 + lanes].astype(bf16)
            raw = dot(spread_heads(keys), queries, 1, 1)
            parts = []
            for head in range(4):
                scores = raw[PAD * head : PAD * (head + 1)] * (LOG2E * 32**-0.5) + (
                    bias[4 * tile + head] + masked
                )
                powers = jnp.exp2(scores - jnp.max(scores, axis=0, keepdims=True))
                total = jnp.sum(powers, axis=0, keepdims=True)
                parts.append((powers * (1.0 / total)).astype(bf16))
            stacked = jnp.concatenate(parts, axis=0)
            probs[window, 4 * PAD * tile : 4 * PAD * (tile + 1), :] = stacked
            mixed_s[at, lanes : lanes + 128] = dot(stacked, spread_heads(values), 0, 0)
        return 0

    lax.fori_loop(0, GROUP, attend, 0)
    mixed_low = mixed_s[...].astype(bf16)
    mixed[...] = mixed_low
    total = rows_s[...] + dot(mixed_low, proj[...]) + proj_bias[...]
    middle[...] = total
    unit, _ = norm_parts(total)
    normed_two[...] = (unit * gain_two[...] + shift_two[...]).astype(bf16)


def rows_kernel(last_start, upper, lower, out, total, rows_s):
    part = pl.program_id(1)

    @pl.when((pl.program_id(0) == 0) & (part == 0))
    def _():
        total[...] = jnp.zeros_like(total)

    def load(window, _):
        at = pl.ds(pl.multiple_of(window * PAD, 8), PAD)
        rows_s[at, :] = window_rows(upper, lower, part * GROUP + window, last_start)
        return 0

    lax.fori_loop(0, GROUP, load, 0)
    rows = rows_s[...]
    out[...] = rows.astype(bf16)
    total[...] += jnp.sum(rows, axis=0, keepdims=True)


def ff_kernel(normed, upstream, up, up_bias, down, active, hidden_grad, up_grad, down_grad, up_bias_grad):
    @pl.when(pl.program_id(0) == 0)
    def _():
        up_grad[...] = jnp.zeros_like(up_grad)
        down_grad[...] = jnp.zeros_like(down_grad)
        up_bias_grad[...] = jnp.zeros_like(up_bias_grad)

    hidden = dot(normed[...], up[...]) + up_bias[...]
    below = 0.5 + 0.5 * lax.erf(hidden * (2.0**-0.5))
    active_low = (hidden * below).astype(bf16)
    active[...] = active_low
    slope = below + hidden * (jnp.exp2(hidden * hidden * (-0.5 * LOG2E)) * 0.3989422804014327)
    grad_low = (slope * dot(upstream[...], down[...], 1, 1)).astype(bf16)
    hidden_grad[...] = grad_low
    up_bias_grad[...] += jnp.sum(grad_low.astype(f32), axis=0, keepdims=True)
    up_grad[...] += dot(normed[...], grad_low, 0, 0)
    down_grad[...] += dot(active_low, upstream[...], 0, 0)


def backward_kernel(*refs):
    count = FF_PARTS
    actives, hidden_grads = refs[:count], refs[count : 2 * count]
    (
        upstream, middle, mixed, inputs, normed_one, joined, probs, up, down, down_bias, proj, qkv, gain_one, gain_two,
        result, input_grad, qkv_grad, qkv_sums, bias_grad, proj_grad, proj_sums, gain_one_grad, shift_one_grad,
        gain_two_grad, shift_two_grad, mixed_grad_s, joined_s,
    ) = refs[2 * count :]

    @pl.when(pl.program_id(0) == 0)
    def _():
        for ref in (qkv_grad, qkv_sums, bias_grad, proj_grad, proj_sums, gain_one_grad, shift_one_grad,
                    gain_two_grad, shift_two_grad):
            ref[...] = jnp.zeros_like(ref)

    def column_sum(values):
        return jnp.sum(values, axis=0, keepdims=True)

    active = jnp.concatenate([ref[...] for ref in actives], axis=1)
    hidden_grad = jnp.concatenate([ref[...] for ref in hidden_grads], axis=1)
    result[...] = middle[...] + dot(active, down[...]) + down_bias[...]
    normed_grad = dot(hidden_grad, up[...], 1, 1)
    unit, rstd = norm_parts(middle[...])
    gain_two_grad[...] += column_sum(normed_grad * unit)
    shift_two_grad[...] += column_sum(normed_grad)
    middle_grad = norm_pull(normed_grad, unit, rstd, gain_two[...]) + upstream[...].astype(f32)
    input_grad[...] = middle_grad
    branch_low = middle_grad.astype(bf16)
    proj_sums[...] += column_sum(branch_low.astype(f32))
    proj_grad[...] += dot(mixed[...], branch_low, 0, 0)
    mixed_grad_s[...] = dot(branch_low, proj[...], 1, 1)

    def attend(window, _):
        at = pl.ds(pl.multiple_of(window * PAD, 8), PAD)
        for tile in range(4):
            lanes = 128 * tile
            queries = joined[window, :, lanes : lanes + 128]
            keys = joined[window, :, 512 + lanes : 640 + lanes]
            values = joined[window, :, 1024 + lanes : 1152 + lanes]
            grad = mixed_grad_s[at, lanes : lanes + 128].astype(bf16)
            probs_grad = dot(spread_heads(values), grad, 1, 1)
            probs_low = probs[window, 4 * PAD * tile : 4 * PAD * (tile + 1), :]
            parts = []
            for head in range(4):
                here = slice(PAD * head, PAD * (head + 1))
                prob = probs_low[here].astype(f32)
                product = prob * probs_grad[here]
                score_grad = product - prob * jnp.sum(product, axis=0, keepdims=True)
                bias_grad[4 * tile + head] += score_grad
                parts.append((score_grad * 32**-0.5).astype(bf16))
            draw = jnp.concatenate(parts, axis=0)
            joined_s[at, lanes : lanes + 128] = dot(draw, spread_heads(keys), 0, 0)
            joined_s[at, 512 + lanes : 640 + lanes] = gather_heads(dot(draw, queries))
            joined_s[at, 1024 + lanes : 1152 + lanes] = gather_heads(dot(probs_low, grad))
        return 0

    lax.fori_loop(0, GROUP, attend, 0)
    joined_low = joined_s[...].astype(bf16)
    qkv_sums[...] += column_sum(joined_low.astype(f32))
    qkv_grad[...] += dot(normed_one[...], joined_low, 0, 0)
    normed_grad = dot(joined_low, qkv[...], 1, 1)
    unit, rstd = norm_parts(inputs[...].astype(f32))
    gain_one_grad[...] += column_sum(normed_grad * unit)
    shift_one_grad[...] += column_sum(normed_grad)
    input_grad[...] += norm_pull(normed_grad, unit, rstd, gain_one[...])


def grid_kernel(windows, out):
    count, _, width = windows.shape
    for row in range(WIN):
        start = WIN * row // 8 * 8
        offset = WIN * row - start
        slab = windows[:, start : start + 16, :].reshape(count * 16, width).astype(bf16)
        col = lax.broadcasted_iota(jnp.int32, (count * WIN, count * 16), 0)
        lane = lax.broadcasted_iota(jnp.int32, (count * WIN, count * 16), 1)
        window = (col * 205) >> 11
        hot = (lane == col + (16 - WIN) * window + offset).astype(f32).astype(bf16)
        out[row] = dot(hot, slab).astype(bf16)


def from_behind(value, axis, steps):
    count = lax.axis_size(axis)
    pairs = [(source, (source + steps) % count) for source in range(count)]
    return lax.ppermute(value, axis, pairs)


def padded(grid):
    below = from_behind(grid[:SHIFT], "row", -1)
    grid = jnp.concatenate((grid, below), axis=0)
    right = from_behind(grid[:, :SHIFT], "col", -1)
    spare = -(grid.shape[1] + SHIFT) % 16
    zeros = jnp.zeros((grid.shape[0], spare, grid.shape[2]), grid.dtype)
    return jnp.concatenate((grid, right, zeros), axis=1)


def roll_out(grid):
    lower = from_behind(grid[-SHIFT:], "row", 1)
    grid = jnp.concatenate((lower, grid[:-SHIFT]), axis=0)
    rightmost = from_behind(grid[:, -SHIFT:], "col", 1)
    return jnp.concatenate((rightmost, grid[:, :-SHIFT]), axis=1)


def relative_index():
    places = jnp.arange(PLACES, dtype=jnp.int32)
    prow, pcol = places // WIN, places % WIN
    return (prow[None, :] - prow[:, None] + WIN - 1) * (2 * WIN - 1) + (pcol[None, :] - pcol[:, None] + WIN - 1)


def body(
    patches, region_ids, qkv_weight, query_bias, value_bias, bias_table, proj_weight, proj_bias, gain_one, shift_one,
    gain_two, shift_two, up_weight, up_bias, down_weight, down_bias, cotangent,
):
    local_rows, local_cols, width = patches.shape
    heads = bias_table.shape[1]
    hidden_units = up_weight.shape[1]
    wrows, wcols = local_rows // WIN, local_cols // WIN
    windows = wrows * wcols
    tokens = windows * PAD
    steps = wcols // GROUP
    padded_patches = padded(patches)
    padded_upstream = padded(cotangent)
    last_start = padded_patches.shape[1] - SLAB
    labels = region_ids.reshape(wrows, WIN, wcols, WIN).transpose(0, 2, 1, 3).reshape(windows, PLACES)
    labels = jnp.pad(labels, ((0, 0), (0, PAD - PLACES)), constant_values=-1)
    onehot = (
        relative_index().reshape(-1)[:, None] == jnp.arange(bias_table.shape[0], dtype=jnp.int32)[None, :]
    ).astype(f32)
    position_bias = jnp.dot(onehot, bias_table, precision=lax.Precision.HIGHEST)
    position_bias = position_bias.reshape(PLACES, PLACES, heads).transpose(2, 0, 1) * LOG2E
    position_bias = jnp.pad(position_bias, ((0, 0), (0, 0), (0, PAD - PLACES)))
    position_bias = jnp.pad(position_bias, ((0, 0), (0, PAD - PLACES), (0, 0)), constant_values=far_below)
    qkv_low, proj_low = qkv_weight.astype(bf16), proj_weight.astype(bf16)
    up_low, down_low = up_weight.astype(bf16), down_weight.astype(bf16)
    qkv_bias = jnp.concatenate((query_bias, jnp.zeros_like(query_bias), value_bias))[None]
    row = lambda vector: vector[None]

    def struct(shape, dtype):
        return jax.ShapeDtypeStruct(shape, dtype)

    def token_spec(columns):
        return pl.BlockSpec((ROWS, columns), lambda i, j: (i * steps + j, 0))

    halo_specs = [
        pl.BlockSpec((SHIFT,) + padded_patches.shape[1:], lambda i, j: (2 * i + 1, 0, 0)),
        pl.BlockSpec((SHIFT,) + padded_patches.shape[1:], lambda i, j: (2 * i + 2, 0, 0)),
    ]
    window_spec = lambda *shape: pl.BlockSpec((GROUP,) + shape, lambda i, j: (i * steps + j,) + (0,) * len(shape))
    operands = (
        position_bias, qkv_low, qkv_bias, proj_low, row(proj_bias), row(gain_one), row(shift_one), row(gain_two),
        row(shift_two),
    )
    inputs, normed_one, joined, probs, mixed, middle, normed_two = pl.pallas_call(
        functools.partial(forward_kernel, last_start),
        grid=(wrows, steps),
        in_specs=halo_specs + [window_spec(1, PAD), window_spec(PAD, 1)] + [whole(a) for a in operands],
        out_specs=[
            token_spec(width), token_spec(width), window_spec(PAD, 3 * width), window_spec(heads * PAD, PAD),
            token_spec(width), token_spec(width), token_spec(width),
        ],
        out_shape=[
            struct((tokens, width), bf16), struct((tokens, width), bf16), struct((windows, PAD, 3 * width), bf16),
            struct((windows, heads * PAD, PAD), bf16), struct((tokens, width), bf16), struct((tokens, width), f32),
            struct((tokens, width), bf16),
        ],
        scratch_shapes=[
            pltpu.VMEM((ROWS, width), f32), pltpu.VMEM((ROWS, 3 * width), f32), pltpu.VMEM((ROWS, width), f32),
        ],
        compiler_params=params(),
    )(padded_patches, padded_patches, labels[:, None, :], labels[:, :, None], *operands)
    upstream, down_bias_grad = pl.pallas_call(
        functools.partial(rows_kernel, last_start),
        grid=(wrows, steps),
        in_specs=halo_specs,
        out_specs=[token_spec(width), pl.BlockSpec((1, width), lambda i, j: (0, 0))],
        out_shape=[struct((tokens, width), bf16), struct((1, width), f32)],
        scratch_shapes=[pltpu.VMEM((ROWS, width), f32)],
        compiler_params=params(),
    )(padded_upstream, padded_upstream)
    part = hidden_units // FF_PARTS
    ff = []
    rows_of = lambda columns: pl.BlockSpec((ROWS, columns), lambda i: (i, 0))
    fixed = lambda *shape: pl.BlockSpec(shape, lambda i: (0,) * len(shape))
    for index in range(FF_PARTS):
        ff.append(
            pl.pallas_call(
                ff_kernel,
                grid=(tokens // ROWS,),
                in_specs=[
                    rows_of(width), rows_of(width),
                    pl.BlockSpec((width, part), lambda i, index=index: (0, index)),
                    pl.BlockSpec((1, part), lambda i, index=index: (0, index)),
                    pl.BlockSpec((part, width), lambda i, index=index: (index, 0)),
                ],
                out_specs=[rows_of(part), rows_of(part), fixed(width, part), fixed(part, width), fixed(1, part)],
                out_shape=[
                    struct((tokens, part), bf16), struct((tokens, part), bf16), struct((width, part), f32),
                    struct((part, width), f32), struct((1, part), f32),
                ],
                compiler_params=params(),
            )(normed_two, upstream, up_low, row(up_bias), down_low)
        )
    actives, hidden_grads, up_grads, down_grads, up_bias_grads = zip(*ff)
    operands = (up_low, down_low, row(down_bias), proj_low, qkv_low, row(gain_one), row(gain_two))
    win_of = lambda *shape: pl.BlockSpec((GROUP,) + shape, lambda i: (i,) + (0,) * len(shape))
    sums = [
        struct((width, 3 * width), f32), struct((1, 3 * width), f32), struct((heads, PAD, PAD), f32),
        struct((width, width), f32),
    ] + [struct((1, width), f32)] * 5
    result, input_grad, *sums = pl.pallas_call(
        backward_kernel,
        grid=(tokens // ROWS,),
        in_specs=[rows_of(part)] * (2 * FF_PARTS)
        + [rows_of(width)] * 5
        + [win_of(PAD, 3 * width), win_of(heads * PAD, PAD)]
        + [whole(a) for a in operands],
        out_specs=[rows_of(width)] * 2 + [whole(a) for a in sums],
        out_shape=[struct((tokens, width), f32)] * 2 + sums,
        scratch_shapes=[pltpu.VMEM((ROWS, width), f32), pltpu.VMEM((ROWS, 3 * width), f32)],
        compiler_params=params(),
    )(*actives, *hidden_grads, upstream, middle, mixed, inputs, normed_one, joined, probs, *operands)
    (qkv_grad, qkv_sums, bias_grad, proj_grad, proj_sums, gain_one_grad, shift_one_grad, gain_two_grad,
     shift_two_grad) = sums

    def to_grid(values):
        return pl.pallas_call(
            grid_kernel,
            grid=(wrows,),
            in_specs=[pl.BlockSpec((wcols, PAD, width), lambda i: (i, 0, 0))],
            out_specs=pl.BlockSpec((WIN, local_cols, width), lambda i: (i, 0, 0)),
            out_shape=struct((local_rows, local_cols, width), bf16),
            compiler_params=params(),
        )(values.reshape(windows, PAD, width))

    block_out = roll_out(to_grid(result))
    patches_grad = roll_out(to_grid(input_grad))
    terms = bias_grad[:, :PLACES, :PLACES].reshape(heads, -1)
    table_grad = lax.dot_general(
        onehot, terms, (((0,), (1,)), ((), ())), precision=lax.Precision.HIGHEST, preferred_element_type=f32
    )
    summed = lax.psum(
        (
            qkv_grad, qkv_sums[0, :width], qkv_sums[0, 2 * width :], table_grad, proj_grad, proj_sums[0],
            gain_one_grad[0], shift_one_grad[0], gain_two_grad[0], shift_two_grad[0],
            jnp.concatenate(up_grads, axis=1), jnp.concatenate(up_bias_grads, axis=1)[0],
            jnp.concatenate(down_grads, axis=0), down_bias_grad[0],
        ),
        ("row", "col"),
    )
    return (block_out, patches_grad) + tuple(summed)


def solution(mesh):
    grid = P("row", "col", None)
    return jax.shard_map(
        body,
        mesh=mesh,
        in_specs=(grid, P("row", "col")) + (P(),) * 14 + (grid,),
        out_specs=(grid, grid) + (P(),) * 14,
        check_vma=False,
    )
```

time: 742 us -> 505 us (0.68)
  matrix products: 241 us -> 13.1 us
  Pallas kernels: 0 us -> 175 us
  local copies, waits for them, and re-layouts: 187 us -> 31.6 us
  other arithmetic: 103 us -> 25.3 us
  blocking collectives: 38.5 us -> 66.3 us
  waiting for transfers between devices: 140 us -> 166 us
    dot_general x19 -> x1, matrix products: 233 us -> 6.24 us  [body(): lax.dot_general(onehot, terms, (((0,), (1,)), ((), ())), precision=lax.Pr...]
    pallas_call x0 -> x9, Pallas kernels: none -> 175 us  [the longest x1 67.7 us: body(): pl.pallas_call(backward_kernel, grid=(tokens // ROWS,), in_specs=[rows_of...]
    convert_element_type x17 -> x0, local copies, waits for them, and re-layouts: 114 us -> none  [the longest x2 34.1 us: body(): joined_grad_low = jnp.stack((queries_grad, keys_grad, values_grad), axis=...]
    psum x1, waiting for transfers between devices: 89 us -> 159 us  [body(): lax.psum((qkv_grad, qkv_sums[0, :width], qkv_sums[0, 2 * width:], table_g...]
    ppermute x4 -> x8, waiting for transfers between devices: 50.6 us -> 7.2 us  [from_behind(): return lax.ppermute(value, axis, pairs)]
    sub x1 -> x0, other arithmetic: 35.6 us -> none  [body(): probs_grad - jnp.sum(probs_grad * probs_again, axis=-1, keepdims=True)]
    reduce_sum x9 -> x0, other arithmetic: 33.9 us -> none  [the longest x1 11.4 us: body(): row_total = jnp.sum(exp_scores, axis=-1, keepdims=True)]
    psum x1, blocking collectives: 38.5 us -> 66.3 us  [body(): lax.psum((qkv_grad, qkv_sums[0, :width], qkv_sums[0, 2 * width:], table_g...]
  transfers between devices with their start and end apart: 5 -> 9, of which waited for: 4 -> 5; matrix products, arithmetic and copies ran while one was open for 13% -> 9% of each run, Pallas kernels for 0% -> 2%
where the time goes in v1:
time: 505 us; the launch traced here: 504 us
  Pallas kernels  175 us (35%)
  waiting for transfers between devices  166 us (33%)
  blocking collectives  66.3 us (13%)
  local copies, waits for them, and re-layouts  31.6 us (6%)
  other arithmetic  25.3 us (5%)
  between operations  14.5 us (3%)
  matrix products  13.1 us (3%)
  starting transfers between devices  11.9 us (2%)
    psum x1, waiting for transfers between devices, body(): lax.psum((qkv_grad, qkv_sums[0, :width], qkv_sums[0, 2 * width:], table_g...  159 us
    pallas_call x1, Pallas kernels, body(): pl.pallas_call(backward_kernel, grid=(tokens // ROWS,), in_specs=[rows_of...  67.7 us
    psum x1, blocking collectives, body(): lax.psum((qkv_grad, qkv_sums[0, :width], qkv_sums[0, 2 * width:], table_g...  66.3 us
    pallas_call x4, Pallas kernels, body(): pl.pallas_call(ff_kernel, grid=(tokens // ROWS,), in_specs=[rows_of(width...  46.9 us
    pallas_call x1, Pallas kernels, body(): pl.pallas_call(functools.partial(forward_kernel, last_start), grid=(wrows...  43.8 us
    unnamed x72, local copies, waits for them, and re-layouts  14 us
    ppermute x8, starting transfers between devices, from_behind(): return lax.ppermute(value, axis, pairs)  11.8 us
  transfers between devices with their start and end apart: 9, of which 5 were waited for; matrix products, arithmetic and copies ran while one was open for 9% of the time, Pallas kernels for 2%

profile of v1, /device:TPU:0, one launch (start us, length us, event | category | flops | bytes accessed | tf_op | source)
XLA Modules:
  0.0 503.8 jit_solution(9015911813801723386)
XLA Ops:
  8.4 6.1 %collective-permute-start.2 = (bf16[5,120,512]{2,1,0:T(8,128)(2,1)S(1)}, bf16[5,120,512]{2,1,0:T(8,128)(2,1)S(1)}, u32[]{:S(2)}, u32[]{:S(2)}) collective-permute-start(bf16[5,120,512]{2,1,0:T(8,128)(2,1)S(1)} %slice.47), channel_id=1, source_target_pairs={{0,28},{4,0},{8,4},{12,8},{16,12},{20,16},{24,20},{28,24},{1,29},{... | collective-permute-start | bytes 1843208 | tf_op jit(solution)/shard_map/ppermute | solution.py:265
  14.4 1.9 slice.45
  17.2 6.9 %fusion.2 = f32[10000,16]{0,1:T(8,128)S(1)} fusion(f32[361,16]{0,1:T(8,128)S(1)} %copy-done, s32[10000]{0:T(1024)S(1)} %add.95), kind=kOutput, calls=%fused_computation.3 | convolution fusion | flops 696889984 | bytes 703104 | tf_op jit(solution)/shard_map/dot_general | solution.py:309
  28.7 3.4 convert_element_type.15.qkv.refs_19_
  38.6 2.2 collective-permute-done
  42.1 1.8 collective-permute-start.3
  45.3 2.2 collective-permute-done.3
  47.5 4.4 maximum_maximum_fusion.1
  52.0 8.5 %shard_map.289 = (bf16[2496,512]{1,0:T(8,128)(2,1)}, f32[1,512]{1,0:T(1,128)}) custom-call(bf16[25,128,512]{2,1,0:T(8,128)(2,1)} %get-tuple-element.114.upper.lower, bf16[25,128,512]{2,1,0:T(8,128)(2,1)} %get-tuple-element.114.upper.lower), custom_call_target="tpu_custom_call" | custom-call | tf_op jit(solution)/shard_map/pallas_call | solution.py:351
  60.5 43.8 %shard_map.288 = (bf16[2496,512]{1,0:T(8,128)(2,1)}, bf16[2496,512]{1,0:T(8,128)(2,1)}, bf16[24,104,1536]{2,1,0:T(8,128)(2,1)}, bf16[24,1664,104]{2,1,0:T(8,128)...) custom-call(bf16[25,128,512]{2,1,0:T(8,128)(2,1)} %get-tuple-element.115.upper.lower, ...), custom_call_target="tpu_custom_call" | custom-call | tf_op jit(solution)/shard_map/pallas_call | solution.py:333
  104.2 11.7 %shard_map.293 = (bf16[2496,512]{1,0:T(8,128)(2,1)}, bf16[2496,512]{1,0:T(8,128)(2,1)}, f32[512,512]{1,0:T(8,128)}, f32[512,512]{1,0:T(8,128)}, f32[1,512]{1,0:T(1,128)}) custom-call(bf16[2496,512]{1,0:T(8,128)(2,1)} %get-tuple-element.56.normed, bf16[2496,512]{1,0:T(8,128)(2,1)} %get-tuple-element.57.upstream.refs_8_, ...), custom_call_target="tpu_custom_call" | custom-call | tf_op jit(solution)/shard_map/pallas_call | solution.py:366
  115.9 11.7 %shard_map.292 = (bf16[2496,512]{1,0:T(8,128)(2,1)}, bf16[2496,512]{1,0:T(8,128)(2,1)}, f32[512,512]{1,0:T(8,128)}, f32[512,512]{1,0:T(8,128)}, f32[1,512]{1,0:T(1,128)}) custom-call(bf16[2496,512]{1,0:T(8,128)(2,1)} %get-tuple-element.56.normed, bf16[2496,512]{1,0:T(8,128)(2,1)} %get-tuple-element.57.upstream.refs_8_, ...), custom_call_target="tpu_custom_call" | custom-call | tf_op jit(solution)/shard_map/pallas_call | solution.py:366
  127.6 11.7 %shard_map.291 = (bf16[2496,512]{1,0:T(8,128)(2,1)}, bf16[2496,512]{1,0:T(8,128)(2,1)}, f32[512,512]{1,0:T(8,128)}, f32[512,512]{1,0:T(8,128)}, f32[1,512]{1,0:T(1,128)}) custom-call(bf16[2496,512]{1,0:T(8,128)(2,1)} %get-tuple-element.56.normed, bf16[2496,512]{1,0:T(8,128)(2,1)} %get-tuple-element.57.upstream.refs_8_, ...), custom_call_target="tpu_custom_call" | custom-call | tf_op jit(solution)/shard_map/pallas_call | solution.py:366
  139.3 11.8 %shard_map.290 = (bf16[2496,512]{1,0:T(8,128)(2,1)}, bf16[2496,512]{1,0:T(8,128)(2,1)}, f32[512,512]{1,0:T(8,128)}, f32[512,512]{1,0:T(8,128)}, f32[1,512]{1,0:T(1,128)}) custom-call(bf16[2496,512]{1,0:T(8,128)(2,1)} %get-tuple-element.56.normed, bf16[2496,512]{1,0:T(8,128)(2,1)} %get-tuple-element.57.upstream.refs_8_, ...), custom_call_target="tpu_custom_call" | custom-call | tf_op jit(solution)/shard_map/pallas_call | solution.py:366
  151.2 3.8 pad_maximum_fusion
  155.0 2.5 pad_maximum_fusion.1
  157.5 67.7 %shard_map.294 = (f32[2496,512]{1,0:T(8,128)}, f32[2496,512]{1,0:T(8,128)}, f32[512,1536]{1,0:T(8,128)}, f32[1,1536]{1,0:T(1,128)}, f32[16,104,104]{2,1,0:T(8,12...) custom-call(bf16[2496,512]{1,0:T(8,128)(2,1)} %get-tuple-element.58., ...), custom_call_target="tpu_custom_call" | custom-call | tf_op jit(solution)/shard_map/pallas_call | solution.py:390
  225.2 4.0 shard_map.295
  229.3 4.0 shard_map.296
  233.3 2.2 slice.64
  235.5 1.9 slice.62
  241.6 2.3 reshape.131
  243.9 6.2 %fusion = f32[361,16]{0,1:T(8,128)S(1)} fusion(f32[16,10000]{1,0:T(8,128)} %reshape.131, s32[10000]{0:T(1024)S(1)} %add.95), kind=kOutput, calls=%fused_computation.1 | convolution fusion | flops 696729984 | bytes 703104 | tf_op jit(solution)/shard_map/dot_general | solution.py:418
  250.2 66.3 %all-reduce.3 = (f32[512]{0:T(512)}, f32[512]{0:T(512)}, f32[361,16]{0,1:T(8,128)}, f32[512]{0:T(512)}, f32[512]{0:T(512)}, /*index=5*/f32[512]{0:T(512)}, f32[5...) all-reduce(f32[512]{0:T(512)S(1)} %bitcast.42, ...), channel_id=1, replica_groups=mesh['row'=8,'col'=4] {'row','col'}, use_global_device_ids=true, to_apply=%region_1.2 | all-reduce | flops 11920 | bytes 95360 | tf_op jit(solution)/shard_map/psum | solution.py:421
  317.7 2.3 collective-permute-start.7
  320.0 2.4 collective-permute-done.5
  322.4 2.5 fusion.6
  324.9 2.5 fusion.5
  327.3 159.0 %all-reduce.7.cloned.1.call-done = (f32[512,1536]{1,0:T(8,128)}, f32[512,512]{1,0:T(8,128)}, f32[512,2048]{1,0:T(8,128)}, f32[2048,512]{1,0:T(8,128)}) async-done(((f32[512,1536]{1,0:T(8,128)}, f32[512,512]{1,0:T(8,128)}, f32[512,2048]{1,0:T(8,128)}, f32[2048,512]{1,0:T(8,128)}), (f32[512,1536]{1,0:T(8,128)}, f32[512,512]{1,0:T(8,128)}, f32[512,2048]{1,0:T(8,128)}, ...) | async-done | bytes 12582928 | tf_op jit(solution)/shard_map/psum | solution.py:421
  486.4 3.9 copy.44
  491.2 2.1 copy.46
  494.9 2.0 copy.47
  (111 shorter events, 23.7 us)
Async XLA Ops:
  7.2 9.9 %copy-start = (f32[361,16]{0,1:T(8,128)S(1)}, f32[361,16]{0,1:T(8,128)}, u32[]{:S(2)}) copy-start(f32[361,16]{0,1:T(8,128)} %param.22) | copy-start | bytes 69316
  7.2 479.1 %all-reduce.7.cloned.1.call-start = ((), (), s32[]{:S(2)}) async-start(), calls=%async_computation | async-start | bytes 25165824 | tf_op jit(solution)/shard_map/psum | solution.py:421
  8.4 33.7 %collective-permute-start.2 = (bf16[5,120,512]{2,1,0:T(8,128)(2,1)S(1)}, bf16[5,120,512]{2,1,0:T(8,128)(2,1)S(1)}, u32[]{:S(2)}, u32[]{:S(2)}) collective-permute-start(bf16[5,120,512]{2,1,0:T(8,128)(2,1)S(1)} %slice.47), channel_id=1, source_target_pairs={{0,28},{4,0},{8,4},{12,8},{16,12},{20,16},{24,20},{28,24},{1,29},{... | collective-permute-start | bytes 1843208 | tf_op jit(solution)/shard_map/ppermute | solution.py:265
  16.4 24.4 %collective-permute-start = (bf16[5,120,512]{2,1,0:T(8,128)(2,1)}, bf16[5,120,512]{2,1,0:T(8,128)(2,1)}, u32[]{:S(2)}, u32[]{:S(2)}) collective-permute-start(bf16[5,120,512]{2,1,0:T(8,128)(2,1)} %slice.45), channel_id=1, source_target_pairs={{0,28},{4,0},{8,4},{12,8},{16,12},{20,16},{24,20},{28,24},{1,29},{... | collective-permute-start | bytes 1843208 | tf_op jit(solution)/shard_map/ppermute | solution.py:265
  17.1 6.9 %copy-start.21 = (f32[512]{0:T(512)S(1)}, f32[512]{0:T(512)}, u32[]{:S(2)}) copy-start(f32[512]{0:T(512)} %param.21) | copy-start | bytes 6148
  17.1 6.9 %copy-start.22 = (f32[512]{0:T(512)S(1)}, f32[512]{0:T(512)}, u32[]{:S(2)}) copy-start(f32[512]{0:T(512)} %param.20) | copy-start | bytes 6148
  17.1 7.5 %copy-start.19 = (s32[20,120]{1,0:T(8,128)S(1)}, s32[20,120]{1,0:T(8,128)}, u32[]{:S(2)}) copy-start(s32[20,120]{1,0:T(8,128)} %param.18) | copy-start | bytes 28804
  17.1 8.1 %copy-start.10 = (f32[512,512]{1,0:T(8,128)S(1)}, f32[512,512]{1,0:T(8,128)}, u32[]{:S(2)}) copy-start(f32[512,512]{1,0:T(8,128)} %param.23) | copy-start | bytes 3145732
  41.9 3.4 collective-permute-start.1
  42.1 5.4 %collective-permute-start.3 = (bf16[25,5,512]{2,1,0:T(8,128)(2,1)S(1)}, bf16[25,5,512]{2,1,0:T(8,128)(2,1)S(1)}, u32[]{:S(2)}, u32[]{:S(2)}) collective-permute-start(bf16[25,5,512]{2,1,0:T(8,128)(2,1)S(1)} %slice.61), channel_id=1, source_target_pairs={{0,3},{1,0},{2,1},{3,2},{4,7},{5,4},{6,5},{7,6},{8,11},{9,8},{10,9... | collective-permute-start | bytes 384008 | tf_op jit(solution)/shard_map/ppermute | solution.py:265
  139.3 11.9 %copy-start.13 = (f32[512,512]{1,0:T(8,128)S(1)}, f32[512,512]{1,0:T(8,128)}, u32[]{:S(2)}) copy-start(f32[512,512]{1,0:T(8,128)} %get-tuple-element.86) | copy-start | bytes 3145732
  139.3 11.9 %copy-start.15 = (f32[512,512]{1,0:T(8,128)S(1)}, f32[512,512]{1,0:T(8,128)}, u32[]{:S(2)}) copy-start(f32[512,512]{1,0:T(8,128)} %get-tuple-element.85) | copy-start | bytes 3145732
  139.3 11.9 %copy-start.17 = (f32[512,512]{1,0:T(8,128)S(1)}, f32[512,512]{1,0:T(8,128)}, u32[]{:S(2)}) copy-start(f32[512,512]{1,0:T(8,128)} %get-tuple-element.84) | copy-start | bytes 3145732
  151.2 3.8 copy-start.12
  151.2 3.8 copy-start.14
  151.2 3.8 copy-start.16
  229.3 9.2 %copy-start.20 = (f32[1,1536]{1,0:T(1,128)S(1)}, f32[1,1536]{1,0:T(1,128)}, u32[]{:S(2)}) copy-start(f32[1,1536]{1,0:T(1,128)} %get-tuple-element.75) | copy-start | bytes 18436
  233.3 6.8 %copy-start.3 = (bf16[20,120,512]{2,1,0:T(8,128)(2,1)S(1)}, bf16[20,120,512]{2,1,0:T(8,128)(2,1)}, u32[]{:S(2)}) copy-start(bf16[20,120,512]{2,1,0:T(8,128)(2,1)} %shard_map.295) | copy-start | bytes 7372804
  237.5 79.1 %collective-permute-start.4 = (bf16[5,120,512]{2,1,0:T(8,128)(2,1)}, bf16[5,120,512]{2,1,0:T(8,128)(2,1)S(1)}, u32[]{:S(2)}, u32[]{:S(2)}) collective-permute-start(bf16[5,120,512]{2,1,0:T(8,128)(2,1)} %slice.62), channel_id=1, source_target_pairs={{0,4},{4,8},{8,12},{12,16},{16,20},{20,24},{24,28},{28,0},{1,5},{5... | collective-permute-start | bytes 1843208 | tf_op jit(solution)/shard_map/ppermute | solution.py:265
  237.7 80.0 %collective-permute-start.6 = (bf16[5,120,512]{2,1,0:T(8,128)(2,1)}, bf16[5,120,512]{2,1,0:T(8,128)(2,1)S(1)}, u32[]{:S(2)}, u32[]{:S(2)}) collective-permute-start(bf16[5,120,512]{2,1,0:T(8,128)(2,1)} %slice.64), channel_id=1, source_target_pairs={{0,4},{4,8},{8,12},{12,16},{16,20},{20,24},{24,28},{28,0},{1,5},{5... | collective-permute-start | bytes 1843208 | tf_op jit(solution)/shard_map/ppermute | solution.py:265
  241.5 8.6 %copy-start.23 = (f32[1,512]{1,0:T(1,128)S(1)}, f32[1,512]{1,0:T(1,128)}, u32[]{:S(2)}) copy-start(f32[1,512]{1,0:T(1,128)} %get-tuple-element.95) | copy-start | bytes 6148
  241.5 8.7 %copy-start.24 = (f32[1,512]{1,0:T(1,128)S(1)}, f32[1,512]{1,0:T(1,128)}, u32[]{:S(2)}) copy-start(f32[1,512]{1,0:T(1,128)} %get-tuple-element.78) | copy-start | bytes 6148
  241.5 8.7 %copy-start.25 = (f32[1,512]{1,0:T(1,128)S(1)}, f32[1,512]{1,0:T(1,128)}, u32[]{:S(2)}) copy-start(f32[1,512]{1,0:T(1,128)} %get-tuple-element.79) | copy-start | bytes 6148
  241.5 8.7 %copy-start.26 = (f32[1,512]{1,0:T(1,128)S(1)}, f32[1,512]{1,0:T(1,128)}, u32[]{:S(2)}) copy-start(f32[1,512]{1,0:T(1,128)} %get-tuple-element.80) | copy-start | bytes 6148
  241.5 8.7 %copy-start.27 = (f32[1,512]{1,0:T(1,128)S(1)}, f32[1,512]{1,0:T(1,128)}, u32[]{:S(2)}) copy-start(f32[1,512]{1,0:T(1,128)} %get-tuple-element.81) | copy-start | bytes 6148
  241.6 8.7 %copy-start.28 = (f32[1,512]{1,0:T(1,128)S(1)}, f32[1,512]{1,0:T(1,128)}, u32[]{:S(2)}) copy-start(f32[1,512]{1,0:T(1,128)} %get-tuple-element.82) | copy-start | bytes 6148
  316.5 5.9 %copy-start.2 = (bf16[15,120,512]{2,1,0:T(8,128)(2,1)S(1)}, bf16[15,120,512]{2,1,0:T(8,128)(2,1)}, u32[]{:S(2)}) copy-start(bf16[15,120,512]{2,1,0:T(8,128)(2,1)} %slice.63) | copy-start | bytes 5529604
  317.6 4.8 collective-permute-start.5
  317.7 7.1 %collective-permute-start.7 = (bf16[20,5,512]{2,1,0:T(8,128)(2,1)S(1)}, bf16[20,5,512]{2,1,0:T(8,128)(2,1)S(1)}, u32[]{:S(2)}, u32[]{:S(2)}) collective-permute-start(bf16[20,5,512]{2,1,0:T(8,128)(2,1)S(1)} %pad_maximum_fusion.4), channel_id=1, source_target_pairs={{0,1},{1,2},{2,3},{3,0},{4,5},{5,6},{6,7},{7,4},{8,9},{9,10},{10,1... | collective-permute-start | bytes 307208 | tf_op jit(solution)/shard_map/ppermute | solution.py:265
  486.3 3.9 copy-start.11
  486.3 4.9 copy-start.7
  491.2 5.7 %copy-start.1 = (f32[361,16]{0,1:T(8,128)S(1)}, f32[361,16]{0,1:T(8,128)}, u32[]{:S(2)}) copy-start(f32[361,16]{0,1:T(8,128)} %param.22) | copy-start | bytes 69316
  (10 other events, 33.1 us)
Sparse Core Ops, SparseCore 0:
  225.3 260.9 all-reduce.6
